TPU v7x, 32 devices: a whole 2x2x4 slice. The times are simulated.
32 devices in a mesh: rows: 8 (over z, x), table: 4 (over y, core).
Axes of the slice: x: 2, y: 2, z: 4, core: 2. Of those that a mesh axis runs over, the one named last changes fastest.
Arguments:
- item_table: bfloat16 [524288, 128], P(('rows', 'table')), may hold values from -40 to 40, as said below
- user_rows: float32 [2048, 128], P(('rows', 'table')), may hold values from -3 to 3
- link_rows: int32 [2048, 128], P(('rows', 'table')), may hold values from 0 to 16383
- link_slots: int32 [2048, 128], P(('rows', 'table')), may hold values from 0 to 8191, as said below
- link_weights: int32 [2048, 128], P(('rows', 'table')), may hold values from 1 to 63
- link_counts: int32 [2048], P(('rows', 'table')), may hold values from 1 to 128
Outputs:
- solved_rows: float32 [2048, 128], P(('rows', 'table'))
Inputs may be any that keep to these rules, and one draw needn't show every extreme that they name: `item_table`: rows differ in scale; values lie within the stated bounds. `link_slots`: on each device (flat index over rows then table, users in blocks of 64), its 8192 entries hold every number of 0 to 8191 exactly once; entry s names slot s % 256 toward the device of flat index s // 256, which holds the linked item, so every device names exactly 256 slots of every owner, live or not.
All inputs are finite; a program needn't handle non-finite values.
Results may differ from a plain program's by a relative error of at most 0.0019.
Values may be sent and summed in bfloat16 or wider, within the bound.
A program may use at most 64 MiB of HBM per device.

v0:
```python
import math

import jax
import jax.numpy as jnp
from jax import lax
from jax.sharding import PartitionSpec as P

CG_STEPS = 3


def refine(apply_system, target, initial):
    estimate = initial
    residual = target - apply_system(estimate)
    direction = residual
    norm_now = jnp.sum(residual * residual, axis=1, keepdims=True)
    for iteration in range(CG_STEPS):
        image = apply_system(direction)
        curvature = jnp.sum(direction * image, axis=1, keepdims=True)
        step_len = norm_now / (curvature + 1e-06)
        estimate = estimate + step_len * direction
        residual = residual - step_len * image
        norm_next = jnp.sum(residual * residual, axis=1, keepdims=True)
        direction = residual + norm_next / (norm_now + 1e-06) * direction
        norm_now = norm_next
    return estimate


def place_requests(slots_flat, rows_flat, block_rows):
    total = slots_flat.shape[0]
    row_pair = jnp.stack([rows_flat // 128, rows_flat % 128], axis=1).astype(jnp.bfloat16)

    def place_one_block(start):
        wanted = start + jnp.arange(block_rows, dtype=jnp.int32)
        selector = (wanted[:, None] == slots_flat[None, :]).astype(jnp.bfloat16)
        picked = jnp.dot(selector, row_pair, preferred_element_type=jnp.float32).astype(jnp.int32)
        return picked[:, 0] * 128 + picked[:, 1]

    starts = jnp.arange(total // block_rows, dtype=jnp.int32) * block_rows
    return lax.map(place_one_block, starts).reshape(total)


def order_rows(slots_flat, arrived, block_rows):
    total = slots_flat.shape[0]
    positions = jnp.arange(total, dtype=jnp.int32)

    def order_one_block(slot_block):
        selector = (slot_block[:, None] == positions[None, :]).astype(jnp.bfloat16)
        return jnp.dot(selector, arrived, preferred_element_type=jnp.float32).astype(jnp.bfloat16)

    return lax.map(order_one_block, slots_flat.reshape(total // block_rows, block_rows)).reshape(
        total, arrived.shape[1]
    )


def per_device(item_table, user_rows, link_rows, link_slots, link_weights, link_counts):
    user_count, features = user_rows.shape
    slot_count = link_rows.shape[1]
    row_groups = lax.axis_size("rows")
    table_groups = lax.axis_size("table")
    devices = row_groups * table_groups
    capacity = user_count * slot_count // devices
    total_items = item_table.shape[0] * devices
    link_total = user_count * slot_count
    block_rows = math.gcd(link_total, 512)
    partial_value = jnp.dot(item_table.T, item_table, preferred_element_type=jnp.float32)
    gramian = lax.psum(partial_value, ("rows", "table"))
    shared = gramian * (slot_count / total_items) + 0.5 * slot_count * jnp.eye(
        features, dtype=jnp.float32
    )
    slots_flat = link_slots.reshape(link_total)
    requests = place_requests(slots_flat, link_rows.reshape(link_total), block_rows)
    outgoing = requests.reshape(devices, capacity)
    arrived = lax.all_to_all(
        item_table[
            lax.all_to_all(outgoing, ("rows", "table"), split_axis=0, concat_axis=0, tiled=True)
        ],
        ("rows", "table"),
        split_axis=0,
        concat_axis=0,
        tiled=True,
    )
    arrived = arrived.reshape(link_total, features)
    fetched = order_rows(slots_flat, arrived, block_rows)
    block_size = math.gcd(user_count, 64)
    block_count = user_count // block_size

    def solve_block(pieces):
        rows_block, weight_block, count_block, start_block = pieces
        live_mask = jnp.arange(slot_count, dtype=jnp.int32)[None, :] < count_block[:, None]
        confidence = jnp.where(live_mask, 1.0 + weight_block.astype(jnp.float32) / 8.0, 0.0)
        scaled = (confidence[:, :, None] * rows_block.astype(jnp.float32)).astype(jnp.bfloat16)
        target = jnp.sum(scaled.astype(jnp.float32), axis=1)
        weighted = jnp.einsum(
            "ulk,ulm->ukm", scaled, rows_block, preferred_element_type=jnp.float32
        )
        system = shared[None, :, :] + weighted

        def apply_system(vector):
            return jnp.einsum("ukm,um->uk", system, vector, precision=lax.Precision.HIGHEST)

        return refine(apply_system, target, start_block)

    solved = lax.map(
        solve_block,
        (
            fetched.reshape(block_count, block_size, slot_count, features),
            link_weights.reshape(block_count, block_size, slot_count),
            link_counts.reshape(block_count, block_size),
            user_rows.reshape(block_count, block_size, features),
        ),
    )
    return solved.reshape(user_count, features)


def solution(mesh):
    placed = (
        P(("rows", "table"), None),
        P(("rows", "table"), None),
        P(("rows", "table"), None),
        P(("rows", "table"), None),
        P(("rows", "table"), None),
        P(("rows", "table")),
    )
    return jax.shard_map(
        per_device,
        mesh=mesh,
        in_specs=placed,
        out_specs=P(("rows", "table"), None),
        check_vma=False,
    )
```

profile of v0, /device:TPU:0, one launch (start us, length us, event | category | flops | bytes accessed | tf_op | source)
XLA Modules:
  0.0 365.9 jit_solution(4394044475449593512)
XLA Ops:
  7.6 77.5 %while.25 = (s32[]{:T(128)}, s32[16,512]{1,0:T(8,128)S(1)}, s32[16]{0:T(128)S(1)}, s32[64,128]{1,0:T(8,128)}, bf16[8192,2]{0,1:T(2,128)(2,1)S(1)}, /*index=5*/s32[]{:T(128)}, s32[]{:T(128)}) while((s32[]{:T(128)}, s32[16,512]{1,0:T(8,128)S(1)}, s32[16]{0:T(128)S(1)}, s32[64,128]{1,0:T(8,128)}, bf16[8192,2]{0,1:T(2,128)(2,1)S(1)}, ...), condition=%wide.region_1.2_spmd, body=%wide.region_0.0_spmd.sunk | while | flops 20974080 | bytes 84065 | solution.py:39
  13.8 3.4 fusion.48
  23.5 3.4 fusion.48
  47.8 3.4 fusion.48
  57.4 3.4 fusion.48
  67.1 3.4 fusion.48
  85.2 14.4 %all_to_all.17 = s32[32,1,256]{2,1,0:T(1,128)S(1)} all-to-all(s32[32,1,256]{2,1,0:T(1,128)S(1)} %all_to_all.11), channel_id=1, replica_groups=mesh['rows'=8,'table'=4] {'rows','table'}, dimensions={0} | all-to-all | bytes 65536 | tf_op jit(solution)/shard_map/all_to_all | solution.py:75
  99.6 30.7 %gather_fusion = bf16[8192,128]{1,0:T(8,128)(2,1)} fusion(bf16[16384,128]{1,0:T(8,128)(2,1)} %param.10, s32[8192]{0:T(1024)S(1)} %broadcast_clamp_fusion), kind=kCustom, calls=%fused_computation | custom fusion | bytes 4227072 | tf_op jit(solution)/shard_map/gather | solution.py:74
  133.2 5.4 %fusion.30 = f32[128,128]{1,0:T(8,128)} fusion(bf16[16384,128]{1,0:T(8,128)(2,1)} %param.10), kind=kOutput, calls=%fused_computation.64 | convolution fusion | flops 536870912 | bytes 4259840 | tf_op jit(solution)/shard_map/dot_general | solution.py:65
  138.7 127.9 %all-reduce.2.cloned.1.call-done = f32[128,128]{1,0:T(8,128)} async-done(((f32[128,128]{1,0:T(8,128)}), f32[128,128]{1,0:T(8,128)}) %all-reduce.2.cloned.1.call-update) | async-done | bytes 65552 | tf_op jit(solution)/shard_map/psum | solution.py:66
  267.4 56.4 %while.26 = (s32[]{:T(128)}, bf16[16,512,128]{2,1,0:T(8,128)(2,1)}, s32[16,512]{1,0:T(8,128)S(1)}, bf16[8192,128]{1,0:T(8,128)(2,1)S(1)}, s32[]{:T(128)}) while((s32[]{:T(128)}, bf16[16,512,128]{2,1,0:T(8,128)(2,1)}, s32[16,512]{1,0:T(8,128)S(1)}, bf16[8192,128]{1,0:T(8,128)(2,1)S(1)}, s32[]{:T(128)}) %tuple.47), condition=%wide.region_3.4_spmd.clone, body=%wide.region_2.3_spmd.clone.sunk | while | flops 1078001664 | bytes 2234945 | solution.py:50
  267.4 3.5 fusion.51
  271.0 3.5 fusion.51
  274.5 3.5 fusion.51
  278.0 3.5 fusion.51
  281.5 3.5 fusion.51
  285.1 3.5 fusion.51
  288.6 3.5 fusion.51
  292.1 3.5 fusion.51
  295.6 3.5 fusion.51
  299.2 3.5 fusion.51
  302.7 3.5 fusion.51
  306.2 3.5 fusion.51
  309.7 3.5 fusion.51
  313.3 3.5 fusion.51
  316.8 3.5 fusion.51
  320.3 3.5 fusion.51
  323.8 3.4 copy.8
  330.7 6.6 %fusion.21 = f32[64,1,128]{2,1,0:T(1,128)S(1)} fusion(f32[64,128,1]{1,2,0:T(1,128)S(1)} %bitcast.70, f32[64,128,128]{2,1,0:T(8,128)S(1)} %fusion.27, f32[128,128]{1,0:T(8,128)S(1)} %select_add_fusion), kind=kOutput, calls=%fused_computation.26 | convolution fusion | flops 13631488 | bytes 4325376 | tf_op jit(solution)/shard_map/while/body/eval_jaxpr/ukm,um->uk/dot_general | solution.py:99
  337.3 6.6 %fusion.19 = f32[64,1,128]{2,1,0:T(1,128)S(1)} fusion(f32[64,128,1]{1,2,0:T(1,128)S(1)} %bitcast.62, f32[64,128,128]{2,1,0:T(8,128)S(1)} %fusion.27, f32[128,128]{1,0:T(8,128)S(1)} %select_add_fusion), kind=kOutput, calls=%fused_computation.24 | convolution fusion | flops 13631488 | bytes 4325376 | tf_op jit(solution)/shard_map/while/body/eval_jaxpr/ukm,um->uk/dot_general | solution.py:99
  344.4 6.8 %fusion.17 = f32[64,1,128]{2,1,0:T(1,128)S(1)} fusion(f32[64,128,1]{1,2,0:T(1,128)S(1)} %bitcast.63, f32[64,128,128]{2,1,0:T(8,128)S(1)} %fusion.27, f32[128,128]{1,0:T(8,128)S(1)} %select_add_fusion), kind=kOutput, calls=%fused_computation.22 | convolution fusion | flops 13631488 | bytes 4325376 | tf_op jit(solution)/shard_map/while/body/eval_jaxpr/ukm,um->uk/dot_general | solution.py:99
  351.6 6.6 %fusion.15 = f32[64,1,128]{2,1,0:T(1,128)S(1)} fusion(f32[64,128,1]{1,2,0:T(1,128)S(1)} %bitcast.64, f32[64,128,128]{2,1,0:T(8,128)S(1)} %fusion.27, f32[128,128]{1,0:T(8,128)S(1)} %select_add_fusion), kind=kOutput, calls=%fused_computation.20 | convolution fusion | flops 13631488 | bytes 4325376 | tf_op jit(solution)/shard_map/while/body/eval_jaxpr/ukm,um->uk/dot_general | solution.py:99
  (131 shorter events, 70.1 us)
Async XLA Ops:
  130.3 137.1 %all-to-all-start.1 = ((bf16[32,256,128]{2,1,0:T(8,128)(2,1)}), bf16[32,256,128]{2,1,0:T(8,128)(2,1)S(1)}, u32[]{:S(2)}, u32[]{:S(2)}) async-start(bf16[32,256,128]{2,1,0:T(8,128)(2,1)} %bitcast.6), calls=%async_computation.1 | async-start | bytes 4194304 | tf_op jit(solution)/shard_map/all_to_all | solution.py:73
  133.1 5.5 %copy-start.1 = (s32[64,128]{1,0:T(8,128)S(1)}, s32[64,128]{1,0:T(8,128)}, u32[]{:S(2)}) copy-start(s32[64,128]{1,0:T(8,128)} %param.14) | copy-start | bytes 98308
  133.1 5.5 %copy-start.3 = (s32[64]{0:T(128)S(1)}, s32[64]{0:T(128)}, u32[]{:S(2)}) copy-start(s32[64]{0:T(128)} %param.15) | copy-start | bytes 772
  133.1 5.6 %copy-start.2 = (s32[64,128]{1,0:T(8,128)S(1)}, s32[64,128]{1,0:T(8,128)}, u32[]{:S(2)}) copy-start(s32[64,128]{1,0:T(8,128)} %get-tuple-element.213) | copy-start | bytes 98308
  133.1 133.4 %all-reduce.2.cloned.1.call-start = ((), (), s32[]{:S(2)}) async-start(), calls=%async_computation.2 | async-start | bytes 131072 | tf_op jit(solution)/shard_map/psum | solution.py:66
  327.2 3.5 copy-start
Sparse Core Ops, SparseCore 0:
  139.5 126.9 all-reduce.1
where the time goes:
time: 369 us; the launch traced here: 366 us
  matrix products  145 us (39%)
  waiting for transfers between devices  128 us (35%)
  local copies, waits for them, and re-layouts  46 us (12%)
  other arithmetic  16.1 us (4%)
  blocking collectives  14.4 us (4%)
  between operations  13.6 us (4%)
    psum x1, waiting for transfers between devices, per_device(): gramian = lax.psum(partial_value, ('rows', 'table'))  128 us
    dot_general x16, matrix products, order_one_block(): jnp.dot(selector, arrived, preferred_element_type=jnp.float32)  56.3 us
    dot_general x16, matrix products, place_one_block(): jnp.dot(selector, row_pair, preferred_element_type=jnp.float32)  54 us
    gather x1, local copies, waits for them, and re-layouts, per_device(): item_table[lax.all_to_all(outgoing, ('rows', 'table'), split_axis=0, conc...  30.7 us
    dot_general x4, matrix products, apply_system(): jnp.einsum('ukm,um->uk', system, vector, precision=lax.Precision.HIGHEST)  26.6 us
    all_to_all x1, blocking collectives, per_device(): lax.all_to_all(outgoing, ('rows', 'table'), split_axis=0, concat_axis=0,...  14.4 us
    add x16, other arithmetic, place_one_block(): wanted = start + jnp.arange(block_rows, dtype=jnp.int32)  11 us
    dynamic_slice x16, local copies, waits for them, and re-layouts, place_requests(): return lax.map(place_one_block, starts).reshape(total)  10.7 us
  transfers between devices with their start and end apart: 2, of which 1 were waited for; matrix products, arithmetic and copies ran while one was open for 2% of the time, Pallas kernels for 0%

commit v1 on v0

v1 whole, which is shorter than its diff:
```python
import functools

import jax
import jax.numpy as jnp
from jax import lax
from jax.experimental import pallas as pl
from jax.experimental.pallas import tpu as pltpu
from jax.sharding import PartitionSpec as P

CG_STEPS = 3
MESH = pl.DeviceIdType.MESH
VMEM_BYTES = 50 * 1024 * 1024
NT = (((1,), (1,)), ((), ()))
TN = (((0,), (0,)), ((), ()))


def position():
    width = lax.axis_size("table")
    count = lax.axis_size("rows") * width
    return lax.axis_index("rows") * width + lax.axis_index("table"), count, width


def partner(step):
    me, count, width = position()
    other = lax.rem(me + step, count)
    return other, (other // width, lax.rem(other, width))


def greet_all():
    _, count, _ = position()
    barrier = pltpu.get_barrier_semaphore()

    def greet(step, carry):
        pl.semaphore_signal(barrier, inc=1, device_id=partner(step)[1], device_id_type=MESH)
        return carry

    lax.fori_loop(1, count, greet, 0)
    pl.semaphore_wait(barrier, count - 1)


def for_partners(body):
    _, count, _ = position()

    def step_body(step, carry):
        body(*partner(step))
        return carry

    lax.fori_loop(1, count, step_body, 0)


def place_requests(slots_ref, rows_ref, owners, capacity):
    users, width = slots_ref.shape
    shift = capacity.bit_length() - 1
    group = 8

    def one_group(index, total):
        at = pl.ds(pl.multiple_of(index * group, group), group)
        slots, rows = slots_ref[at, :], rows_ref[at, :]
        owner, inner = slots >> shift, slots & (capacity - 1)
        high, low = (rows >> 7).astype(jnp.float32), (rows & 127).astype(jnp.float32)
        for user in range(group):
            pick = slice(user, user + 1)
            match = lax.broadcasted_iota(jnp.int32, (owners, width), 0) == owner[pick]
            left = jnp.concatenate(
                [jnp.where(match, high[pick], 0.0), jnp.where(match, low[pick], 0.0)], axis=0
            ).astype(jnp.bfloat16)
            hit = lax.broadcasted_iota(jnp.int32, (capacity, width), 0) == inner[pick]
            right = jnp.where(hit, 1.0, 0.0).astype(jnp.bfloat16)
            total = total + lax.dot_general(left, right, NT, preferred_element_type=jnp.float32)
        return total

    total = lax.fori_loop(
        0, users // group, one_group, jnp.zeros((2 * owners, capacity), jnp.float32)
    )
    return (total[:owners] * 128.0 + total[owners:]).astype(jnp.int32)


def request_kernel(slots_ref, rows_ref, asked_ref, wanted, send_sem, recv_sem):
    me, count, _ = position()
    capacity = wanted.shape[2]
    wanted[...] = place_requests(slots_ref, rows_ref, count, capacity)[:, None, :]
    greet_all()

    def copy(other, device):
        return pltpu.make_async_remote_copy(
            src_ref=wanted.at[other], dst_ref=asked_ref.at[me],
            send_sem=send_sem.at[other], recv_sem=recv_sem.at[me],
            device_id=device, device_id_type=MESH,
        )

    def landing(other, device):
        return pltpu.make_async_remote_copy(
            src_ref=wanted.at[other], dst_ref=asked_ref.at[other],
            send_sem=send_sem.at[other], recv_sem=recv_sem.at[other],
            device_id=device, device_id_type=MESH,
        )

    for_partners(lambda other, device: copy(other, device).start())
    asked_ref[me] = wanted[me]
    for_partners(lambda other, device: landing(other, device).wait())


def table_pass(table_ref, wide, features):
    chunk = 1024

    def one_chunk(index, total):
        at = pl.ds(pl.multiple_of(index * chunk, chunk), chunk)
        block = table_ref[at, :]
        wide[at, :] = block.astype(jnp.float32)
        return total + lax.dot_general(block, block, TN, preferred_element_type=jnp.float32)

    return lax.fori_loop(
        0, table_ref.shape[0] // chunk, one_chunk, jnp.zeros((features, features), jnp.float32)
    )


def gather_rows(read_index, source, target, base, amount):
    group = 32

    def one_group(index, carry):
        start = index * group
        values = [source[pl.ds(read_index(start + i), 1), :] for i in range(group)]
        for i, value in enumerate(values):
            target[pl.ds(base + start + i, 1), :] = value
        return carry

    lax.fori_loop(0, amount // group, one_group, 0)


def gather_kernel(asked_ref, table_ref, rows_ref, gram_ref, wide, stage):
    owners, _, capacity = asked_ref.shape
    features = table_ref.shape[1]
    share = features // owners
    gram = table_pass(table_ref, wide, features)
    for index in range(owners):
        gram_ref[index] = gram[index * share:(index + 1) * share]

    def one_block(other, carry):
        gather_rows(lambda i: asked_ref[other, 0, i], wide, stage, 0, capacity)
        at = pl.ds(pl.multiple_of(other * capacity, capacity), capacity)
        rows_ref[at, :] = stage[...].astype(jnp.bfloat16)
        return carry

    lax.fori_loop(0, owners, one_block, 0)


def exchange_kernel(
    rows_ref, gram_ref, arrived_ref, whole_ref, partial, summed, sems, part_sems, whole_sems
):
    me, count, _ = position()
    capacity = rows_ref.shape[0] // count
    greet_all()

    def block(index):
        return pl.ds(pl.multiple_of(index * capacity, capacity), capacity)

    def part_copy(other, device, slot):
        return pltpu.make_async_remote_copy(
            src_ref=gram_ref.at[other], dst_ref=partial.at[slot],
            send_sem=part_sems.at[0, other], recv_sem=part_sems.at[1, slot],
            device_id=device, device_id_type=MESH,
        )

    def whole_copy(other, device, slot):
        return pltpu.make_async_remote_copy(
            src_ref=summed, dst_ref=whole_ref.at[slot],
            send_sem=whole_sems.at[0, other], recv_sem=whole_sems.at[1, slot],
            device_id=device, device_id_type=MESH,
        )

    def rows_copy(other, device, slot):
        return pltpu.make_async_remote_copy(
            src_ref=rows_ref.at[block(other)], dst_ref=arrived_ref.at[block(slot)],
            send_sem=sems.at[0, other], recv_sem=sems.at[1, slot],
            device_id=device, device_id_type=MESH,
        )

    for_partners(lambda other, device: part_copy(other, device, me).start())
    for_partners(lambda other, device: rows_copy(other, device, me).start())
    partial[me] = gram_ref[me]
    arrived_ref[block(me), :] = rows_ref[block(me), :]
    for_partners(lambda other, device: part_copy(other, device, other).wait())
    summed[...] = jnp.sum(partial[...], axis=0)
    for_partners(lambda other, device: whole_copy(other, device, me).start())
    whole_ref[me] = summed[...]
    for_partners(lambda other, device: rows_copy(other, device, other).wait())
    for_partners(lambda other, device: whole_copy(other, device, other).wait())


def solve_kernel(
    total_items,
    slots_ref, counts_ref, arrived_ref, gram_ref, weights_ref, start_ref, out_ref,
    wide, fetched, scaled, shared, target, vector, image,
):
    users, features = start_ref.shape
    slot_count = weights_ref.shape[1]
    owners, share, _ = gram_ref.shape
    group = 8
    for index in range(owners):
        shared[index * share:(index + 1) * share, :] = gram_ref[index]
    line = lax.broadcasted_iota(jnp.int32, (features, features), 0)
    column = lax.broadcasted_iota(jnp.int32, (features, features), 1)
    shared[...] = shared[...] * (slot_count / total_items) + jnp.where(
        line == column, 0.5 * slot_count, 0.0
    )
    wide[...] = arrived_ref[...].astype(jnp.float32)

    def fetch_user(user, carry):
        base = user * slot_count
        gather_rows(lambda i: slots_ref[user, i], wide, fetched, base, slot_count)
        return carry

    lax.fori_loop(0, users, fetch_user, 0)

    def rows_of(user):
        return pl.ds(pl.multiple_of(user * slot_count, slot_count), slot_count)

    def group_at(index):
        return pl.ds(pl.multiple_of(index * group, group), group)

    def scale_group(index, carry):
        at = group_at(index)
        place = lax.broadcasted_iota(jnp.int32, (group, slot_count), 0)
        limit = jnp.zeros((group, slot_count), jnp.int32)
        for j in range(group):
            limit = jnp.where(place == j, counts_ref[index * group + j], limit)
        live = lax.broadcasted_iota(jnp.int32, (group, slot_count), 1) < limit
        confidence = jnp.where(live, 1.0 + weights_ref[at, :].astype(jnp.float32) / 8.0, 0.0)
        turned = confidence.T
        sums = []
        for j in range(group):
            rows = rows_of(index * group + j)
            product = (turned[:, j:j + 1] * fetched[rows, :]).astype(jnp.bfloat16)
            product = product.astype(jnp.float32)
            scaled[rows, :] = product
            sums.append(jnp.sum(product, axis=0, keepdims=True))
        target[at, :] = jnp.concatenate(sums, axis=0)
        return carry

    lax.fori_loop(0, users // group, scale_group, 0)

    def apply_system(value):
        vector[...] = value

        def apply_group(index, carry):
            at = group_at(index)
            some = vector[at, :]
            images = []
            for j in range(group):
                rows = rows_of(index * group + j)
                inner = jnp.sum(fetched[rows, :] * some[j:j + 1], axis=1, keepdims=True)
                images.append(jnp.sum(scaled[rows, :] * inner, axis=0, keepdims=True))
            image[at, :] = jnp.concatenate(images, axis=0)
            return carry

        lax.fori_loop(0, users // group, apply_group, 0)
        common = lax.dot_general(
            value, shared[...], NT,
            precision=lax.Precision.HIGHEST, preferred_element_type=jnp.float32,
        )
        return common + image[...]

    estimate = start_ref[...]
    residual = target[...] - apply_system(estimate)
    direction = residual
    norm_now = jnp.sum(residual * residual, axis=1, keepdims=True)
    for _ in range(CG_STEPS):
        moved = apply_system(direction)
        curvature = jnp.sum(direction * moved, axis=1, keepdims=True)
        step_len = norm_now / (curvature + 1e-06)
        estimate = estimate + step_len * direction
        residual = residual - step_len * moved
        norm_next = jnp.sum(residual * residual, axis=1, keepdims=True)
        direction = residual + norm_next / (norm_now + 1e-06) * direction
        norm_now = norm_next
    out_ref[...] = estimate


def per_device(item_table, user_rows, link_rows, link_slots, link_weights, link_counts):
    user_count, features = user_rows.shape
    slot_count = link_rows.shape[1]
    devices = lax.axis_size("rows") * lax.axis_size("table")
    link_total = user_count * slot_count
    capacity = link_total // devices
    share = features // devices
    total_items = item_table.shape[0] * devices
    vmem = pl.BlockSpec(memory_space=pltpu.VMEM)
    smem = pl.BlockSpec(memory_space=pltpu.SMEM)
    dma = pltpu.SemaphoreType.DMA
    f32 = jnp.float32

    asked = pl.pallas_call(
        request_kernel,
        out_shape=jax.ShapeDtypeStruct((devices, 1, capacity), jnp.int32),
        in_specs=[vmem, vmem],
        out_specs=vmem,
        scratch_shapes=[
            pltpu.VMEM((devices, 1, capacity), jnp.int32), dma((devices,)), dma((devices,)),
        ],
        compiler_params=pltpu.CompilerParams(
            collective_id=0, has_side_effects=True, vmem_limit_bytes=VMEM_BYTES
        ),
        name="place_and_ask",
    )(link_slots, link_rows)

    rows, gram = pl.pallas_call(
        gather_kernel,
        out_shape=[
            jax.ShapeDtypeStruct((link_total, features), jnp.bfloat16),
            jax.ShapeDtypeStruct((devices, share, features), f32),
        ],
        in_specs=[smem, vmem],
        out_specs=[vmem, vmem],
        scratch_shapes=[
            pltpu.VMEM(item_table.shape, f32), pltpu.VMEM((capacity, features), f32),
        ],
        compiler_params=pltpu.CompilerParams(vmem_limit_bytes=VMEM_BYTES),
        name="gather_and_gramian",
    )(asked, item_table)

    arrived, whole = pl.pallas_call(
        exchange_kernel,
        out_shape=[
            jax.ShapeDtypeStruct((link_total, features), jnp.bfloat16),
            jax.ShapeDtypeStruct((devices, share, features), f32),
        ],
        in_specs=[vmem, vmem],
        out_specs=[vmem, vmem],
        scratch_shapes=[
            pltpu.VMEM((devices, share, features), f32), pltpu.VMEM((share, features), f32),
            dma((2, devices)), dma((2, devices)), dma((2, devices)),
        ],
        compiler_params=pltpu.CompilerParams(
            collective_id=1, has_side_effects=True, vmem_limit_bytes=VMEM_BYTES
        ),
        name="exchange_rows",
    )(rows, gram)

    return pl.pallas_call(
        functools.partial(solve_kernel, total_items),
        out_shape=jax.ShapeDtypeStruct((user_count, features), f32),
        in_specs=[smem, smem, vmem, vmem, vmem, vmem],
        out_specs=vmem,
        scratch_shapes=[
            pltpu.VMEM((link_total, features), f32),
            pltpu.VMEM((link_total, features), f32),
            pltpu.VMEM((link_total, features), f32),
            pltpu.VMEM((features, features), f32),
            pltpu.VMEM((user_count, features), f32),
            pltpu.VMEM((user_count, features), f32),
            pltpu.VMEM((user_count, features), f32),
        ],
        compiler_params=pltpu.CompilerParams(vmem_limit_bytes=VMEM_BYTES),
        name="reorder_and_solve",
    )(link_slots, link_counts, arrived, whole, link_weights, user_rows)


def solution(mesh):
    flat = P(("rows", "table"), None)
    return jax.shard_map(
        per_device,
        mesh=mesh,
        in_specs=(flat, flat, flat, flat, flat, P(("rows", "table"))),
        out_specs=flat,
        check_vma=False,
    )
```

time: 369 us -> 137 us (0.37)
  matrix products: 145 us -> 0 us
  Pallas kernels: 0 us -> 134 us
  waiting for transfers between devices: 128 us -> 0 us
  local copies, waits for them, and re-layouts: 46 us -> 2.87 us
  other arithmetic: 16.1 us -> 0 us
  blocking collectives: 14.4 us -> 0 us
  between operations: 13.6 us -> 0.07 us
    dot_general x38 -> x0, matrix products: 145 us -> none  [the longest x16 56.3 us: order_one_block(): jnp.dot(selector, arrived, preferred_element_type=jnp.float32)]
    pallas_call x0 -> x4, Pallas kernels: none -> 134 us  [the longest x1 63.4 us: per_device(): pl.pallas_call(exchange_kernel, out_shape=[jax.ShapeDtypeStruct((link_tot...]
    psum x1 -> x0, waiting for transfers between devices: 128 us -> none  [per_device(): gramian = lax.psum(partial_value, ('rows', 'table'))]
    gather x1 -> x0, local copies, waits for them, and re-layouts: 30.7 us -> none  [per_device(): item_table[lax.all_to_all(outgoing, ('rows', 'table'), split_axis=0, conc...]
    all_to_all x1 -> x0, blocking collectives: 14.4 us -> none  [per_device(): lax.all_to_all(outgoing, ('rows', 'table'), split_axis=0, concat_axis=0,...]
    add x36 -> x0, other arithmetic: 12.9 us -> none  [the longest x16 11 us: place_one_block(): wanted = start + jnp.arange(block_rows, dtype=jnp.int32)]
    dynamic_slice x32 -> x0, local copies, waits for them, and re-layouts: 10.8 us -> none  [the longest x16 10.7 us: place_requests(): return lax.map(place_one_block, starts).reshape(total)]
  transfers between devices with their start and end apart: 2 -> 0, of which waited for: 1 -> 0; matrix products, arithmetic and copies ran while one was open for 2% -> 0% of each run, Pallas kernels for 0% -> 0%
where the time goes in v1:
time: 137 us
  Pallas kernels  134 us (98%)
  local copies, waits for them, and re-layouts  2.87 us (2%)
    pallas_call x1, Pallas kernels, per_device(): pl.pallas_call(exchange_kernel, out_shape=[jax.ShapeDtypeStruct((link_tot...  63.4 us
    pallas_call x1, Pallas kernels, per_device(): pl.pallas_call(functools.partial(solve_kernel, total_items), out_shape=ja...  32.7 us
    pallas_call x1, Pallas kernels, per_device(): pl.pallas_call(gather_kernel, out_shape=[jax.ShapeDtypeStruct((link_total...  25.4 us
    pallas_call x1, Pallas kernels, per_device(): pl.pallas_call(request_kernel, out_shape=jax.ShapeDtypeStruct((devices, 1...  12.7 us
    unnamed x14, local copies, waits for them, and re-layouts  2.87 us

profile of v1, /device:TPU:0, one launch (start us, length us, event | category | flops | bytes accessed | tf_op | source)
XLA Modules:
  0.0 137.1 jit_solution(7909008654447532745)
XLA Ops:
  0.0 0.0 copy-start.1
  0.0 0.8 copy-done.1
  0.8 0.0 copy-start.5
  0.8 0.8 copy-done.5
  1.5 12.7 %place_and_ask.1.asked_ref = s32[32,1,256]{2,1,0:T(1,128)S(1)} custom-call(s32[64,128]{1,0:T(8,128)S(1)} %copy-done.1, s32[64,128]{1,0:T(8,128)S(1)} %copy-done.5), custom_call_target="tpu_custom_call" | custom-call | tf_op jit(solution)/shard_map/place_and_ask/pallas_call | solution.py:292
  14.2 25.4 %gather_and_gramian.1 = (bf16[8192,128]{1,0:T(8,128)(2,1)S(1)}, f32[32,4,128]{2,1,0:T(4,128)S(1)}) custom-call(s32[32,1,256]{2,1,0:T(1,128)S(1)} %place_and_ask.1.asked_ref, bf16[16384,128]{1,0:T(8,128)(2,1)} %table_ref.1), custom_call_target="tpu_custom_call" | custom-call | tf_op jit(solution)/shard_map/gather_and_gramian/pallas_call | solution.py:306
  39.7 0.0 copy-start
  39.7 1.3 copy-done
  41.0 0.0 copy-start.2
  41.0 0.0 copy-start.3
  41.0 0.0 copy-start.4
  41.0 0.0 copy-start.6
  41.0 63.4 %exchange_rows.1 = (bf16[8192,128]{1,0:T(8,128)(2,1)S(1)}, f32[32,4,128]{2,1,0:T(4,128)S(1)}) custom-call(bf16[8192,128]{1,0:T(8,128)(2,1)} %copy-done, f32[32,4,128]{2,1,0:T(4,128)S(1)} %get-tuple-element.10.gram_ref), custom_call_target="tpu_custom_call" | custom-call | tf_op jit(solution)/shard_map/exchange_rows/pallas_call | solution.py:321
  104.4 0.0 copy-done.2
  104.4 0.0 copy-done.3
  104.5 0.0 copy-done.4
  104.5 0.0 copy-done.6
  104.5 32.7 %reorder_and_solve.1 = f32[64,128]{1,0:T(8,128)} custom-call(s32[64,128]{1,0:T(8,128)S(1)} %copy-done.2, s32[64]{0:T(128)S(1)} %copy-done.6, bf16[8192,128]{1,0:T(8,128)(2,1)S(1)} %get-tuple-element.11.arrived_ref, f32[32,4,128]{2,1,0:T(4,128)S(1)} %get-tuple-element.12.gram_ref, s32[64,128]{1,0:T(8,128)S(1)} %copy-done.3, f32[64,128]{1,0:T(8,128)S(1)} %copy-done.4), custom_call_target="tpu_custom_call" | custom-call | tf_op jit(solution)/shard_map/reorder_and_solve/pallas_call | solution.py:339
Async XLA Ops:
  0.0 0.8 copy-start.1
  0.8 0.8 copy-start.5
  39.7 1.3 copy-start
  41.0 63.4 %copy-start.2 = (s32[64,128]{1,0:T(8,128)S(1)}, s32[64,128]{1,0:T(8,128)}, u32[]{:S(2)}) copy-start(s32[64,128]{1,0:T(8,128)} %slots_ref.3) | copy-start | bytes 98308
  41.0 63.4 %copy-start.3 = (s32[64,128]{1,0:T(8,128)S(1)}, s32[64,128]{1,0:T(8,128)}, u32[]{:S(2)}) copy-start(s32[64,128]{1,0:T(8,128)} %weights_ref.1) | copy-start | bytes 98308
  41.0 63.4 %copy-start.4 = (f32[64,128]{1,0:T(8,128)S(1)}, f32[64,128]{1,0:T(8,128)}, u32[]{:S(2)}) copy-start(f32[64,128]{1,0:T(8,128)} %start_ref.1) | copy-start | bytes 98308
  41.0 63.4 %copy-start.6 = (s32[64]{0:T(128)S(1)}, s32[64]{0:T(128)}, u32[]{:S(2)}) copy-start(s32[64]{0:T(128)} %counts_ref.1) | copy-start | bytes 772

commit v2 on v0

v2 whole, which is shorter than its diff:
```python
import functools

import jax
import jax.numpy as jnp
from jax import lax
from jax.experimental import pallas as pl
from jax.experimental.pallas import tpu as pltpu
from jax.sharding import PartitionSpec as P

CG_STEPS = 3
MESH = pl.DeviceIdType.MESH
VMEM_BYTES = 50 * 1024 * 1024
NT = (((1,), (1,)), ((), ()))
TN = (((0,), (0,)), ((), ()))


def position():
    width = lax.axis_size("table")
    count = lax.axis_size("rows") * width
    return lax.axis_index("rows") * width + lax.axis_index("table"), count, width


def partner(step):
    me, count, width = position()
    away = count // 2 + (1 - 2 * lax.rem(step, 2)) * ((step + 1) // 2)
    later, earlier = lax.rem(me + away, count), lax.rem(me - away + count, count)
    return later, earlier, (later // width, lax.rem(later, width))


def for_partners(body, first=0, last=None):
    _, count, _ = position()

    def step_body(step, carry):
        body(*partner(step))
        return carry

    lax.fori_loop(first, count - 1 if last is None else last, step_body, 0)


def split(value):
    high = value.astype(jnp.bfloat16)
    low = (value - high.astype(jnp.float32)).astype(jnp.bfloat16)
    return jnp.concatenate([high, low], axis=0)


def joined(value):
    half = value.shape[0] // 2
    return value[:half] + value[half:]


def place_links(slots_ref, rows_ref, weights_ref, counts_ref, owners, capacity):
    users, width = slots_ref.shape
    shift = capacity.bit_length() - 1
    group = 8

    def one_group(index, total):
        at = pl.ds(pl.multiple_of(index * group, group), group)
        slots, rows = slots_ref[at, :], rows_ref[at, :]
        owner, inner = slots >> shift, slots & (capacity - 1)
        high, low = (rows >> 7).astype(jnp.float32), (rows & 127).astype(jnp.float32)
        line = lax.broadcasted_iota(jnp.int32, (group, width), 0)
        limit = jnp.zeros((group, width), jnp.int32)
        for j in range(group):
            limit = jnp.where(line == j, counts_ref[index * group + j], limit)
        live = lax.broadcasted_iota(jnp.int32, (group, width), 1) < limit
        confidence = jnp.where(live, 1.0 + weights_ref[at, :].astype(jnp.float32) / 8.0, 0.0)
        member = (line + index * group).astype(jnp.float32)
        for user in range(group):
            pick = slice(user, user + 1)
            match = lax.broadcasted_iota(jnp.int32, (owners, width), 0) == owner[pick]
            left = jnp.concatenate(
                [jnp.where(match, part[pick], 0.0) for part in (high, low, member, confidence)],
                axis=0,
            ).astype(jnp.bfloat16)
            hit = lax.broadcasted_iota(jnp.int32, (capacity, width), 0) == inner[pick]
            right = jnp.where(hit, 1.0, 0.0).astype(jnp.bfloat16)
            total = total + lax.dot_general(left, right, NT, preferred_element_type=jnp.float32)
        return total

    total = lax.fori_loop(
        0, users // group, one_group, jnp.zeros((4 * owners, capacity), jnp.float32)
    )
    high, low, member, confidence = (total[i * owners:(i + 1) * owners] for i in range(4))
    return (high * 128.0 + low).astype(jnp.int32), member, confidence


def gather_rows(read_index, source, target):
    group = 32

    def one_group(index, carry):
        start = index * group
        values = [source[pl.ds(read_index(start + i), 1), :] for i in range(group)]
        for i, value in enumerate(values):
            target[pl.ds(start + i, 1), :] = value
        return carry

    lax.fori_loop(0, target.shape[0] // group, one_group, 0)


def sweep_kernel(
    total_items,
    counts_ref, table_ref, slots_ref, rows_ref, weights_ref, start_ref, out_ref,
    table, wide, wanted, asked, indices, placed, marks, stage, leaving, arrived, scaled,
    parts, partial, summed, whole, shared, image, target,
    table_sem, index_sem, ask_sems, row_sems, part_sems, whole_sems,
):
    me, count, _ = position()
    users, features = start_ref.shape
    slot_count = slots_ref.shape[1]
    capacity = wanted.shape[2]
    share = features // count
    assert wide.shape[0] & (wide.shape[0] - 1) == 0
    f32 = jnp.float32

    def remote(source, landing, sems, outgoing, incoming, device):
        return pltpu.make_async_remote_copy(
            src_ref=source, dst_ref=landing,
            send_sem=sems.at[0, outgoing], recv_sem=sems.at[1, incoming],
            device_id=device, device_id_type=MESH,
        )

    def ask_copy(to, slot, device):
        return remote(wanted.at[to], asked.at[slot], ask_sems, to, slot, device)

    def row_copy(to, slot, device):
        return remote(leaving.at[to], arrived.at[slot], row_sems, to, slot, device)

    def part_copy(to, slot, device):
        return remote(parts.at[to], partial.at[slot], part_sems, to, slot, device)

    def whole_copy(to, slot, device):
        return remote(summed, whole.at[slot], whole_sems, to, slot, device)

    def finish(copy):
        def both(to, source, device):
            copy(to, source, device).wait()

        return both

    load_table = pltpu.make_async_copy(table_ref, table, table_sem)
    load_table.start()
    barrier = pltpu.get_barrier_semaphore()
    for_partners(
        lambda to, source, device: pl.semaphore_signal(
            barrier, inc=1, device_id=device, device_id_type=MESH
        )
    )
    rows, member, confidence = place_links(
        slots_ref, rows_ref, weights_ref, counts_ref, count, capacity
    )
    wanted[...] = rows[:, None, :]
    placed[0] = member[:, None, :]
    placed[1] = confidence[:, None, :]
    pl.semaphore_wait(barrier, count - 1)
    for_partners(lambda to, source, device: ask_copy(to, me, device).start())
    asked[me] = wanted[me]

    def mark(owner, carry):
        line = lax.broadcasted_iota(jnp.int32, (users, capacity), 0)
        hit = line == placed[0, owner].astype(jnp.int32)
        marks[owner] = jnp.where(hit, placed[1, owner], 0.0)
        return carry

    lax.fori_loop(0, count, mark, 0)

    chunk = 1024
    load_table.wait()

    def widen(index, carry):
        at = pl.ds(pl.multiple_of(index * chunk, chunk), chunk)
        wide[at, :] = table[at, :].astype(f32)
        return carry

    lax.fori_loop(0, table.shape[0] // chunk, widen, 0)

    for_partners(finish(ask_copy))
    load_indices = pltpu.make_async_copy(asked, indices, index_sem)
    load_indices.start()
    load_indices.wait()

    def gather_block(owner):
        gather_rows(lambda i: indices[owner, 0, i] & (wide.shape[0] - 1), wide, stage)
        return stage[...].astype(jnp.bfloat16)

    def send_block(to, source, device):
        leaving[to] = gather_block(to)
        row_copy(to, me, device).start()

    for_partners(send_block)
    arrived[me] = gather_block(me)

    def gramian(index, total):
        at = pl.ds(pl.multiple_of(index * chunk, chunk), chunk)
        block = table[at, :]
        return total + lax.dot_general(block, block, TN, preferred_element_type=f32)

    own = lax.fori_loop(
        0, table.shape[0] // chunk, gramian, jnp.zeros((features, features), f32)
    )
    for index in range(count):
        parts[index] = own[index * share:(index + 1) * share]
    for_partners(lambda to, source, device: part_copy(to, me, device).start())
    partial[me] = parts[me]

    def products(owner, vector_parts, total):
        inner = joined(
            lax.dot_general(vector_parts, arrived[owner], NT, preferred_element_type=f32)
        )
        inner = jnp.where(marks[owner] > 0.0, inner, 0.0)
        return total + jnp.dot(split(inner), scaled[owner], preferred_element_type=f32)

    start_parts = split(start_ref[...])
    image[...] = jnp.zeros_like(image)
    target[...] = jnp.zeros_like(target)
    ones = jnp.ones((users, features), jnp.bfloat16)

    def take_block(owner):
        marked = marks[owner]
        spread = lax.dot_general(
            marked.astype(jnp.bfloat16), ones, TN, preferred_element_type=f32
        )
        scaled[owner] = (spread * arrived[owner].astype(f32)).astype(jnp.bfloat16)
        member = jnp.where(marked > 0.0, 1.0, 0.0).astype(jnp.bfloat16)
        target[...] += jnp.dot(member, scaled[owner], preferred_element_type=f32)
        image[...] = products(owner, start_parts, image[...])

    def receive_block(to, source, device):
        row_copy(to, source, device).wait()
        take_block(source)

    take_block(me)
    middle = count // 2
    for_partners(receive_block, 0, middle)
    for_partners(finish(part_copy))
    summed[...] = jnp.sum(partial[...], axis=0)
    for_partners(lambda to, source, device: whole_copy(to, me, device).start())
    whole[me] = summed[...]
    for_partners(receive_block, middle)
    for_partners(finish(whole_copy))

    for index in range(count):
        shared[index * share:(index + 1) * share, :] = whole[index]
    line = lax.broadcasted_iota(jnp.int32, (features, features), 0)
    column = lax.broadcasted_iota(jnp.int32, (features, features), 1)
    shared[...] = shared[...] * (slot_count / total_items) + jnp.where(
        line == column, 0.5 * slot_count, 0.0
    )

    def common(value):
        return lax.dot_general(
            value, shared[...], NT, precision=lax.Precision.HIGHEST, preferred_element_type=f32
        )

    def apply_system(value):
        vector_parts = split(value)
        unroll = 4

        def some(index, total):
            for j in range(unroll):
                total = products(index * unroll + j, vector_parts, total)
            return total

        total = lax.fori_loop(
            0, count // unroll, some, jnp.zeros((2 * users, features), f32)
        )
        return common(value) + joined(total)

    estimate = start_ref[...]
    residual = target[...] - (common(estimate) + joined(image[...]))
    direction = residual
    norm_now = jnp.sum(residual * residual, axis=1, keepdims=True)
    for _ in range(CG_STEPS):
        moved = apply_system(direction)
        curvature = jnp.sum(direction * moved, axis=1, keepdims=True)
        step_len = norm_now / (curvature + 1e-06)
        estimate = estimate + step_len * direction
        residual = residual - step_len * moved
        norm_next = jnp.sum(residual * residual, axis=1, keepdims=True)
        direction = residual + norm_next / (norm_now + 1e-06) * direction
        norm_now = norm_next
    out_ref[...] = estimate


def per_device(item_table, user_rows, link_rows, link_slots, link_weights, link_counts):
    user_count, features = user_rows.shape
    slot_count = link_rows.shape[1]
    devices = lax.axis_size("rows") * lax.axis_size("table")
    capacity = user_count * slot_count // devices
    share = features // devices
    total_items = item_table.shape[0] * devices
    vmem = pl.BlockSpec(memory_space=pltpu.VMEM)
    smem = pl.BlockSpec(memory_space=pltpu.SMEM)
    hbm = pl.BlockSpec(memory_space=pl.ANY)
    dma = pltpu.SemaphoreType.DMA
    f32, bf16, i32 = jnp.float32, jnp.bfloat16, jnp.int32

    return pl.pallas_call(
        functools.partial(sweep_kernel, total_items),
        out_shape=jax.ShapeDtypeStruct((user_count, features), f32),
        in_specs=[smem, hbm, vmem, vmem, vmem, vmem],
        out_specs=vmem,
        scratch_shapes=[
            pltpu.VMEM(item_table.shape, bf16),
            pltpu.VMEM(item_table.shape, f32),
            pltpu.VMEM((devices, 1, capacity), i32),
            pltpu.VMEM((devices, 1, capacity), i32),
            pltpu.SMEM((devices, 1, capacity), i32),
            pltpu.VMEM((2, devices, 1, capacity), f32),
            pltpu.VMEM((devices, user_count, capacity), f32),
            pltpu.VMEM((capacity, features), f32),
            pltpu.VMEM((devices, capacity, features), bf16),
            pltpu.VMEM((devices, capacity, features), bf16),
            pltpu.VMEM((devices, capacity, features), bf16),
            pltpu.VMEM((devices, share, features), f32),
            pltpu.VMEM((devices, share, features), f32),
            pltpu.VMEM((share, features), f32),
            pltpu.VMEM((devices, share, features), f32),
            pltpu.VMEM((features, features), f32),
            pltpu.VMEM((2 * user_count, features), f32),
            pltpu.VMEM((user_count, features), f32),
            dma, dma,
            dma((2, devices)), dma((2, devices)), dma((2, devices)), dma((2, devices)),
        ],
        compiler_params=pltpu.CompilerParams(
            collective_id=0, has_side_effects=True, vmem_limit_bytes=VMEM_BYTES
        ),
        name="sweep",
    )(link_counts, item_table, link_slots, link_rows, link_weights, user_rows)


def solution(mesh):
    flat = P(("rows", "table"), None)
    return jax.shard_map(
        per_device,
        mesh=mesh,
        in_specs=(flat, flat, flat, flat, flat, P(("rows", "table"))),
        out_specs=flat,
        check_vma=False,
    )
```

time: 369 us -> 93.6 us (0.25)
  matrix products: 145 us -> 0 us
  waiting for transfers between devices: 128 us -> 0 us
  Pallas kernels: 0 us -> 88.9 us
  local copies, waits for them, and re-layouts: 46 us -> 4.3 us
  other arithmetic: 16.1 us -> 0 us
  blocking collectives: 14.4 us -> 0 us
  between operations: 13.6 us -> 0.01 us
    dot_general x38 -> x0, matrix products: 145 us -> none  [the longest x16 56.3 us: order_one_block(): jnp.dot(selector, arrived, preferred_element_type=jnp.float32)]
    psum x1 -> x0, waiting for transfers between devices: 128 us -> none  [per_device(): gramian = lax.psum(partial_value, ('rows', 'table'))]
    pallas_call x0 -> x1, Pallas kernels: none -> 88.9 us  [per_device(): pl.pallas_call(functools.partial(sweep_kernel, total_items), out_shape=ja...]
    gather x1 -> x0, local copies, waits for them, and re-layouts: 30.7 us -> none  [per_device(): item_table[lax.all_to_all(outgoing, ('rows', 'table'), split_axis=0, conc...]
    all_to_all x1 -> x0, blocking collectives: 14.4 us -> none  [per_device(): lax.all_to_all(outgoing, ('rows', 'table'), split_axis=0, concat_axis=0,...]
    add x36 -> x0, other arithmetic: 12.9 us -> none  [the longest x16 11 us: place_one_block(): wanted = start + jnp.arange(block_rows, dtype=jnp.int32)]
    dynamic_slice x32 -> x0, local copies, waits for them, and re-layouts: 10.8 us -> none  [the longest x16 10.7 us: place_requests(): return lax.map(place_one_block, starts).reshape(total)]
    unnamed x8 -> x11, local copies, waits for them, and re-layouts: 0.03 us -> 4.3 us
  transfers between devices with their start and end apart: 2 -> 0, of which waited for: 1 -> 0; matrix products, arithmetic and copies ran while one was open for 2% -> 0% of each run, Pallas kernels for 0% -> 0%
where the time goes in v2:
time: 93.6 us; the launch traced here: 93.2 us
  Pallas kernels  88.9 us (95%)
  local copies, waits for them, and re-layouts  4.3 us (5%)
    pallas_call x1, Pallas kernels, per_device(): pl.pallas_call(functools.partial(sweep_kernel, total_items), out_shape=ja...  88.9 us
    unnamed x11, local copies, waits for them, and re-layouts  4.3 us

profile of v2, /device:TPU:0, one launch (start us, length us, event | category | flops | bytes accessed | tf_op | source)
XLA Modules:
  0.0 93.2 jit_solution(5520887594157764931)
XLA Ops:
  0.0 0.0 copy-start
  0.0 0.8 copy-done
  0.8 0.0 copy-start.1
  0.8 0.8 copy-done.1
  1.5 0.0 copy-start.2
  1.5 0.8 copy-done.2
  2.3 0.0 copy-start.3
  2.3 0.8 copy-done.3
  3.0 0.0 copy-start.4
  3.0 0.7 copy-done.4
  3.7 88.9 %sweep.1 = f32[64,128]{1,0:T(8,128)S(1)} custom-call(s32[64]{0:T(128)S(1)} %copy-done.4, bf16[16384,128]{1,0:T(8,128)(2,1)} %table_ref.1, s32[64,128]{1,0:T(8,128)S(1)} %copy-done, s32[64,128]{1,0:T(8,128)S(1)} %copy-done.1, s32[64,128]{1,0:T(8,128)S(1)} %copy-done.2, f32[64,128]{1,0:T(8,128)S(1)} %copy-done.3), custom_call_target="tpu_custom_call" | custom-call | tf_op jit(solution)/shard_map/sweep/pallas_call | solution.py:297
  92.6 0.6 copy.8
Async XLA Ops:
  0.0 0.8 copy-start
  0.8 0.8 copy-start.1
  1.5 0.8 copy-start.2
  2.3 0.8 copy-start.3
  3.0 0.7 copy-start.4

commit v3 on v2

--- a/solution.py
+++ b/solution.py
@@ -9,7 +9,7 @@
 
 CG_STEPS = 3
 MESH = pl.DeviceIdType.MESH
-VMEM_BYTES = 50 * 1024 * 1024
+VMEM_BYTES = 64 * 1024 * 1024 - 65536
 NT = (((1,), (1,)), ((), ()))
 TN = (((0,), (0,)), ((), ()))
 
@@ -22,7 +22,7 @@
 
 def partner(step):
     me, count, width = position()
-    away = count // 2 + (1 - 2 * lax.rem(step, 2)) * ((step + 1) // 2)
+    away = (step + 1) // 2 + lax.rem(step + 1, 2) * (count // 2)
     later, earlier = lax.rem(me + away, count), lax.rem(me - away + count, count)
     return later, earlier, (later // width, lax.rem(later, width))
 
@@ -99,10 +99,10 @@
 
 def sweep_kernel(
     total_items,
-    counts_ref, table_ref, slots_ref, rows_ref, weights_ref, start_ref, out_ref,
-    table, wide, wanted, asked, indices, placed, marks, stage, leaving, arrived, scaled,
+    counts_hbm, table_hbm, slots_hbm, rows_hbm, weights_hbm, start_hbm, out_ref,
+    counts_ref, slots_ref, rows_ref, weights_ref, start_ref, table, wide, wanted, asked, indices, placed, marks, stage, leaving, arrived, scaled,
     parts, partial, summed, whole, shared, image, target,
-    table_sem, index_sem, ask_sems, row_sems, part_sems, whole_sems,
+    input_sems, table_sem, index_sem, ask_sems, row_sems, part_sems, whole_sems,
 ):
     me, count, _ = position()
     users, features = start_ref.shape
@@ -137,7 +137,16 @@
 
         return both
 
-    load_table = pltpu.make_async_copy(table_ref, table, table_sem)
+    loads = [
+        pltpu.make_async_copy(source, landing, input_sems.at[index])
+        for index, (source, landing) in enumerate([
+            (slots_hbm, slots_ref), (rows_hbm, rows_ref), (counts_hbm, counts_ref),
+            (weights_hbm, weights_ref), (start_hbm, start_ref),
+        ])
+    ]
+    for load in loads:
+        load.start()
+    load_table = pltpu.make_async_copy(table_hbm, table, table_sem)
     load_table.start()
     barrier = pltpu.get_barrier_semaphore()
     for_partners(
@@ -145,6 +154,8 @@
             barrier, inc=1, device_id=device, device_id_type=MESH
         )
     )
+    for load in loads:
+        load.wait()
     rows, member, confidence = place_links(
         slots_ref, rows_ref, weights_ref, counts_ref, count, capacity
     )
@@ -289,17 +300,21 @@
     share = features // devices
     total_items = item_table.shape[0] * devices
     vmem = pl.BlockSpec(memory_space=pltpu.VMEM)
-    smem = pl.BlockSpec(memory_space=pltpu.SMEM)
-    hbm = pl.BlockSpec(memory_space=pl.ANY)
+    hbm = pl.BlockSpec(memory_space=pltpu.HBM)
     dma = pltpu.SemaphoreType.DMA
     f32, bf16, i32 = jnp.float32, jnp.bfloat16, jnp.int32
 
     return pl.pallas_call(
         functools.partial(sweep_kernel, total_items),
         out_shape=jax.ShapeDtypeStruct((user_count, features), f32),
-        in_specs=[smem, hbm, vmem, vmem, vmem, vmem],
+        in_specs=[hbm] * 6,
         out_specs=vmem,
         scratch_shapes=[
+            pltpu.SMEM(link_counts.shape, i32),
+            pltpu.VMEM(link_slots.shape, i32),
+            pltpu.VMEM(link_rows.shape, i32),
+            pltpu.VMEM(link_weights.shape, i32),
+            pltpu.VMEM(user_rows.shape, f32),
             pltpu.VMEM(item_table.shape, bf16),
             pltpu.VMEM(item_table.shape, f32),
             pltpu.VMEM((devices, 1, capacity), i32),
@@ -318,7 +333,7 @@
             pltpu.VMEM((features, features), f32),
             pltpu.VMEM((2 * user_count, features), f32),
             pltpu.VMEM((user_count, features), f32),
-            dma, dma,
+            dma((5,)), dma, dma,
             dma((2, devices)), dma((2, devices)), dma((2, devices)), dma((2, devices)),
         ],
         compiler_params=pltpu.CompilerParams(

time: 93.6 us -> 89 us (0.951)
  local copies, waits for them, and re-layouts: 4.3 us -> 1.38 us
  Pallas kernels: 88.9 us -> 87.5 us
    unnamed x11 -> x1, local copies, waits for them, and re-layouts: 4.3 us -> 1.38 us
    pallas_call x1, Pallas kernels: 88.9 us -> 87.5 us  [per_device(): pl.pallas_call(functools.partial(sweep_kernel, total_items), out_shape=ja...]
where the time goes in v3:
time: 89 us; the launch traced here: 88.9 us
  Pallas kernels  87.5 us (98%)
  local copies, waits for them, and re-layouts  1.38 us (2%)
    pallas_call x1, Pallas kernels, per_device(): pl.pallas_call(functools.partial(sweep_kernel, total_items), out_shape=ja...  87.5 us

profile of v3, /device:TPU:0, one launch (start us, length us, event | category | flops | bytes accessed | tf_op | source)
XLA Modules:
  0.0 88.9 jit_solution(5976630785362341558)
XLA Ops:
  0.0 87.5 %sweep.1 = f32[64,128]{1,0:T(8,128)} custom-call(s32[64]{0:T(128)} %counts_hbm.1, bf16[16384,128]{1,0:T(8,128)(2,1)} %table_hbm.1, s32[64,128]{1,0:T(8,128)} %slots_hbm.1, s32[64,128]{1,0:T(8,128)} %rows_hbm.1, s32[64,128]{1,0:T(8,128)} %weights_hbm.1, f32[64,128]{1,0:T(8,128)} %start_hbm.1), custom_call_target="tpu_custom_call" | custom-call | tf_op jit(solution)/shard_map/sweep/pallas_call | solution.py:307
  87.5 1.4 %copy.8 = f32[64,128]{1,0:T(8,128)} copy(f32[64,128]{1,0:T(8,128)} %sweep.1) | data formatting | bytes 65536

commit v4 on v3

--- a/solution.py
+++ b/solution.py
@@ -48,40 +48,36 @@
     return value[:half] + value[half:]
 
 
-def place_links(slots_ref, rows_ref, weights_ref, counts_ref, owners, capacity):
+def place(slots_ref, read_parts, owners, capacity):
     users, width = slots_ref.shape
     shift = capacity.bit_length() - 1
     group = 8
 
     def one_group(index, total):
         at = pl.ds(pl.multiple_of(index * group, group), group)
-        slots, rows = slots_ref[at, :], rows_ref[at, :]
+        slots = slots_ref[at, :]
         owner, inner = slots >> shift, slots & (capacity - 1)
-        high, low = (rows >> 7).astype(jnp.float32), (rows & 127).astype(jnp.float32)
-        line = lax.broadcasted_iota(jnp.int32, (group, width), 0)
-        limit = jnp.zeros((group, width), jnp.int32)
-        for j in range(group):
-            limit = jnp.where(line == j, counts_ref[index * group + j], limit)
-        live = lax.broadcasted_iota(jnp.int32, (group, width), 1) < limit
-        confidence = jnp.where(live, 1.0 + weights_ref[at, :].astype(jnp.float32) / 8.0, 0.0)
-        member = (line + index * group).astype(jnp.float32)
-        for user in range(group):
+        parts = read_parts(index * group, at)
+
+        def choose(user):
             pick = slice(user, user + 1)
             match = lax.broadcasted_iota(jnp.int32, (owners, width), 0) == owner[pick]
-            left = jnp.concatenate(
-                [jnp.where(match, part[pick], 0.0) for part in (high, low, member, confidence)],
-                axis=0,
-            ).astype(jnp.bfloat16)
+            left = jnp.concatenate([jnp.where(match, part[pick], 0.0) for part in parts], axis=0)
             hit = lax.broadcasted_iota(jnp.int32, (capacity, width), 0) == inner[pick]
-            right = jnp.where(hit, 1.0, 0.0).astype(jnp.bfloat16)
-            total = total + lax.dot_general(left, right, NT, preferred_element_type=jnp.float32)
+            return left.astype(jnp.bfloat16), jnp.where(hit, 1.0, 0.0).astype(jnp.bfloat16)
+
+        for user in range(0, group, 2):
+            lefts, rights = zip(choose(user), choose(user + 1))
+            total = total + lax.dot_general(
+                jnp.concatenate(lefts, axis=1), jnp.concatenate(rights, axis=1), NT,
+                preferred_element_type=jnp.float32,
+            )
         return total
 
     total = lax.fori_loop(
-        0, users // group, one_group, jnp.zeros((4 * owners, capacity), jnp.float32)
-    )
-    high, low, member, confidence = (total[i * owners:(i + 1) * owners] for i in range(4))
-    return (high * 128.0 + low).astype(jnp.int32), member, confidence
+        0, users // group, one_group, jnp.zeros((2 * owners, capacity), jnp.float32)
+    )
+    return total[:owners], total[owners:]
 
 
 def gather_rows(read_index, source, target):
@@ -154,17 +150,61 @@
             barrier, inc=1, device_id=device, device_id_type=MESH
         )
     )
-    for load in loads:
+    for load in loads[:2]:
         load.wait()
-    rows, member, confidence = place_links(
-        slots_ref, rows_ref, weights_ref, counts_ref, count, capacity
-    )
-    wanted[...] = rows[:, None, :]
-    placed[0] = member[:, None, :]
-    placed[1] = confidence[:, None, :]
+
+    def row_parts(first, at):
+        rows = rows_ref[at, :]
+        return (rows >> 7).astype(f32), (rows & 127).astype(f32)
+
+    high, low = place(slots_ref, row_parts, count, capacity)
+    wanted[...] = (high * 128.0 + low).astype(jnp.int32)[:, None, :]
     pl.semaphore_wait(barrier, count - 1)
     for_partners(lambda to, source, device: ask_copy(to, me, device).start())
     asked[me] = wanted[me]
+
+    chunk = 1024
+    load_table.wait()
+
+    def widen(index, carry):
+        at = pl.ds(pl.multiple_of(index * chunk, chunk), chunk)
+        wide[at, :] = table[at, :].astype(f32)
+        return carry
+
+    lax.fori_loop(0, table.shape[0] // chunk, widen, 0)
+
+    for_partners(finish(ask_copy))
+    load_indices = pltpu.make_async_copy(asked, indices, index_sem)
+    load_indices.start()
+    load_indices.wait()
+
+    def gather_block(owner):
+        gather_rows(lambda i: indices[owner, 0, i] & (wide.shape[0] - 1), wide, stage)
+        return stage[...].astype(jnp.bfloat16)
+
+    def send_block(to, source, device):
+        leaving[to] = gather_block(to)
+        row_copy(to, me, device).start()
+
+    for_partners(send_block)
+    arrived[me] = gather_block(me)
+
+    for load in loads[2:]:
+        load.wait()
+
+    def link_parts(first, at):
+        shape = (8, slot_count)
+        line = lax.broadcasted_iota(jnp.int32, shape, 0)
+        limit = jnp.zeros(shape, jnp.int32)
+        for j in range(shape[0]):
+            limit = jnp.where(line == j, counts_ref[first + j], limit)
+        live = lax.broadcasted_iota(jnp.int32, shape, 1) < limit
+        confidence = jnp.where(live, 1.0 + weights_ref[at, :].astype(f32) / 8.0, 0.0)
+        return (line + first).astype(f32), confidence
+
+    member, confidence = place(slots_ref, link_parts, count, capacity)
+    placed[0] = member[:, None, :]
+    placed[1] = confidence[:, None, :]
 
     def mark(owner, carry):
         line = lax.broadcasted_iota(jnp.int32, (users, capacity), 0)
@@ -174,32 +214,6 @@
 
     lax.fori_loop(0, count, mark, 0)
 
-    chunk = 1024
-    load_table.wait()
-
-    def widen(index, carry):
-        at = pl.ds(pl.multiple_of(index * chunk, chunk), chunk)
-        wide[at, :] = table[at, :].astype(f32)
-        return carry
-
-    lax.fori_loop(0, table.shape[0] // chunk, widen, 0)
-
-    for_partners(finish(ask_copy))
-    load_indices = pltpu.make_async_copy(asked, indices, index_sem)
-    load_indices.start()
-    load_indices.wait()
-
-    def gather_block(owner):
-        gather_rows(lambda i: indices[owner, 0, i] & (wide.shape[0] - 1), wide, stage)
-        return stage[...].astype(jnp.bfloat16)
-
-    def send_block(to, source, device):
-        leaving[to] = gather_block(to)
-        row_copy(to, me, device).start()
-
-    for_partners(send_block)
-    arrived[me] = gather_block(me)
-
     def gramian(index, total):
         at = pl.ds(pl.multiple_of(index * chunk, chunk), chunk)
         block = table[at, :]
@@ -213,40 +227,54 @@
     for_partners(lambda to, source, device: part_copy(to, me, device).start())
     partial[me] = parts[me]
 
-    def products(owner, vector_parts, total):
+    def products(owner, vector_parts, total, weighted):
         inner = joined(
             lax.dot_general(vector_parts, arrived[owner], NT, preferred_element_type=f32)
         )
         inner = jnp.where(marks[owner] > 0.0, inner, 0.0)
-        return total + jnp.dot(split(inner), scaled[owner], preferred_element_type=f32)
+        return total + jnp.dot(split(inner), weighted, preferred_element_type=f32)
 
     start_parts = split(start_ref[...])
     image[...] = jnp.zeros_like(image)
     target[...] = jnp.zeros_like(target)
     ones = jnp.ones((users, features), jnp.bfloat16)
 
-    def take_block(owner):
-        marked = marks[owner]
-        spread = lax.dot_general(
-            marked.astype(jnp.bfloat16), ones, TN, preferred_element_type=f32
-        )
-        scaled[owner] = (spread * arrived[owner].astype(f32)).astype(jnp.bfloat16)
-        member = jnp.where(marked > 0.0, 1.0, 0.0).astype(jnp.bfloat16)
-        target[...] += jnp.dot(member, scaled[owner], preferred_element_type=f32)
-        image[...] = products(owner, start_parts, image[...])
-
-    def receive_block(to, source, device):
-        row_copy(to, source, device).wait()
-        take_block(source)
-
-    take_block(me)
-    middle = count // 2
-    for_partners(receive_block, 0, middle)
+    def take_blocks(owners):
+        goals, images = target[...], image[...]
+        for owner in owners:
+            marked = marks[owner]
+            spread = lax.dot_general(
+                marked.astype(jnp.bfloat16), ones, TN, preferred_element_type=f32
+            )
+            weighted = (spread * arrived[owner].astype(f32)).astype(jnp.bfloat16)
+            scaled[owner] = weighted
+            member = jnp.where(marked > 0.0, 1.0, 0.0).astype(jnp.bfloat16)
+            goals = goals + jnp.dot(member, weighted, preferred_element_type=f32)
+            images = products(owner, start_parts, images, weighted)
+        target[...] = goals
+        image[...] = images
+
+    def receive_blocks(steps):
+        sources = []
+        for step in steps:
+            to, source, device = partner(step)
+            row_copy(to, source, device).wait()
+            sources.append(source)
+        take_blocks(sources)
+
+    def receive_pair(index, carry):
+        receive_blocks([2 * index + 1, 2 * index + 2])
+        return carry
+
+    take_blocks([me])
+    receive_blocks([0])
+    pairs = (count - 2) // 2
+    lax.fori_loop(0, pairs // 2, receive_pair, 0)
     for_partners(finish(part_copy))
     summed[...] = jnp.sum(partial[...], axis=0)
     for_partners(lambda to, source, device: whole_copy(to, me, device).start())
     whole[me] = summed[...]
-    for_partners(receive_block, middle)
+    lax.fori_loop(pairs // 2, pairs, receive_pair, 0)
     for_partners(finish(whole_copy))
 
     for index in range(count):
@@ -264,11 +292,12 @@
 
     def apply_system(value):
         vector_parts = split(value)
-        unroll = 4
+        unroll = 8
 
         def some(index, total):
             for j in range(unroll):
-                total = products(index * unroll + j, vector_parts, total)
+                owner = index * unroll + j
+                total = products(owner, vector_parts, total, scaled[owner])
             return total
 
         total = lax.fori_loop(

time: 89 us -> 83.1 us (0.934)
  Pallas kernels: 87.5 us -> 81.6 us
    pallas_call x1, Pallas kernels: 87.5 us -> 81.6 us  [per_device(): pl.pallas_call(functools.partial(sweep_kernel, total_items), out_shape=ja...]
where the time goes in v4:
time: 83.1 us; the launch traced here: 83 us
  Pallas kernels  81.6 us (98%)
  local copies, waits for them, and re-layouts  1.38 us (2%)
    pallas_call x1, Pallas kernels, per_device(): pl.pallas_call(functools.partial(sweep_kernel, total_items), out_shape=ja...  81.6 us

profile of v4, /device:TPU:0, one launch (start us, length us, event | category | flops | bytes accessed | tf_op | source)
XLA Modules:
  0.0 83.0 jit_solution(9687024546840225780)
XLA Ops:
  0.0 81.6 %sweep.1 = f32[64,128]{1,0:T(8,128)} custom-call(s32[64]{0:T(128)} %counts_hbm.1, bf16[16384,128]{1,0:T(8,128)(2,1)} %table_hbm.1, s32[64,128]{1,0:T(8,128)} %slots_hbm.1, s32[64,128]{1,0:T(8,128)} %rows_hbm.1, s32[64,128]{1,0:T(8,128)} %weights_hbm.1, f32[64,128]{1,0:T(8,128)} %start_hbm.1), custom_call_target="tpu_custom_call" | custom-call | tf_op jit(solution)/shard_map/sweep/pallas_call | solution.py:336
  81.6 1.4 %copy.8 = f32[64,128]{1,0:T(8,128)} copy(f32[64,128]{1,0:T(8,128)} %sweep.1) | data formatting | bytes 65536

commit v5 on v4

--- a/solution.py
+++ b/solution.py
@@ -22,9 +22,11 @@
 
 def partner(step):
     me, count, width = position()
-    away = (step + 1) // 2 + lax.rem(step + 1, 2) * (count // 2)
-    later, earlier = lax.rem(me + away, count), lax.rem(me - away + count, count)
-    return later, earlier, (later // width, lax.rem(later, width))
+    away = lax.div(step + 1, 2) + lax.rem(step + 1, 2) * (count // 2)
+    later, earlier = me + away, me - away
+    later = jnp.where(later >= count, later - count, later)
+    earlier = jnp.where(earlier < 0, earlier + count, earlier)
+    return later, earlier, (lax.div(later, width), lax.rem(later, width))
 
 
 def for_partners(body, first=0, last=None):
@@ -228,11 +230,11 @@
     partial[me] = parts[me]
 
     def products(owner, vector_parts, total, weighted):
-        inner = joined(
-            lax.dot_general(vector_parts, arrived[owner], NT, preferred_element_type=f32)
-        )
-        inner = jnp.where(marks[owner] > 0.0, inner, 0.0)
-        return total + jnp.dot(split(inner), weighted, preferred_element_type=f32)
+        inner = lax.dot_general(vector_parts, arrived[owner], NT, preferred_element_type=f32)
+        whole_parts = vector_parts.shape[0] == users
+        inner = jnp.where(marks[owner] > 0.0, inner if whole_parts else joined(inner), 0.0)
+        inner_parts = inner.astype(jnp.bfloat16) if whole_parts else split(inner)
+        return total + jnp.dot(inner_parts, weighted, preferred_element_type=f32)
 
     start_parts = split(start_ref[...])
     image[...] = jnp.zeros_like(image)
@@ -290,9 +292,8 @@
             value, shared[...], NT, precision=lax.Precision.HIGHEST, preferred_element_type=f32
         )
 
-    def apply_system(value):
-        vector_parts = split(value)
-        unroll = 8
+    def apply_system(vector_parts):
+        unroll = min(count, 32)
 
         def some(index, total):
             for j in range(unroll):
@@ -300,17 +301,20 @@
                 total = products(owner, vector_parts, total, scaled[owner])
             return total
 
-        total = lax.fori_loop(
-            0, count // unroll, some, jnp.zeros((2 * users, features), f32)
-        )
-        return common(value) + joined(total)
+        nothing = jnp.zeros((vector_parts.shape[0], features), f32)
+        if unroll == count:
+            return some(0, nothing)
+        return lax.fori_loop(0, count // unroll, some, nothing)
 
     estimate = start_ref[...]
     residual = target[...] - (common(estimate) + joined(image[...]))
     direction = residual
     norm_now = jnp.sum(residual * residual, axis=1, keepdims=True)
-    for _ in range(CG_STEPS):
-        moved = apply_system(direction)
+    for step in range(CG_STEPS):
+        if step < CG_STEPS - 1:
+            moved = common(direction) + joined(apply_system(split(direction)))
+        else:
+            moved = common(direction) + apply_system(direction.astype(jnp.bfloat16))
         curvature = jnp.sum(direction * moved, axis=1, keepdims=True)
         step_len = norm_now / (curvature + 1e-06)
         estimate = estimate + step_len * direction

time: 83.1 us -> 81.9 us (0.986)
  Pallas kernels: 81.6 us -> 80.3 us
    pallas_call x1, Pallas kernels: 81.6 us -> 80.3 us  [per_device(): pl.pallas_call(functools.partial(sweep_kernel, total_items), out_shape=ja...]
where the time goes in v5:
time: 81.9 us; the launch traced here: 81.7 us
  Pallas kernels  80.3 us (98%)
  local copies, waits for them, and re-layouts  1.38 us (2%)
    pallas_call x1, Pallas kernels, per_device(): pl.pallas_call(functools.partial(sweep_kernel, total_items), out_shape=ja...  80.3 us

profile of v5, /device:TPU:0, one launch (start us, length us, event | category | flops | bytes accessed | tf_op | source)
XLA Modules:
  0.0 81.7 jit_solution(6378736694476545464)
XLA Ops:
  0.0 80.3 %sweep.1 = f32[64,128]{1,0:T(8,128)} custom-call(s32[64]{0:T(128)} %counts_hbm.1, bf16[16384,128]{1,0:T(8,128)(2,1)} %table_hbm.1, s32[64,128]{1,0:T(8,128)} %slots_hbm.1, s32[64,128]{1,0:T(8,128)} %rows_hbm.1, s32[64,128]{1,0:T(8,128)} %weights_hbm.1, f32[64,128]{1,0:T(8,128)} %start_hbm.1), custom_call_target="tpu_custom_call" | custom-call | tf_op jit(solution)/shard_map/sweep/pallas_call | solution.py:340
  80.3 1.4 %copy.8 = f32[64,128]{1,0:T(8,128)} copy(f32[64,128]{1,0:T(8,128)} %sweep.1) | data formatting | bytes 65536

commit v6 on v5

--- a/solution.py
+++ b/solution.py
@@ -175,20 +175,34 @@
 
     lax.fori_loop(0, table.shape[0] // chunk, widen, 0)
 
-    for_partners(finish(ask_copy))
-    load_indices = pltpu.make_async_copy(asked, indices, index_sem)
-    load_indices.start()
-    load_indices.wait()
-
     def gather_block(owner):
         gather_rows(lambda i: indices[owner, 0, i] & (wide.shape[0] - 1), wide, stage)
         return stage[...].astype(jnp.bfloat16)
 
-    def send_block(to, source, device):
+    def index_copy(owner):
+        return pltpu.make_async_copy(asked.at[owner], indices.at[owner], index_sem.at[owner])
+
+    def fetch_request(step):
+        to, _, device = partner(step)
+        ask_copy(to, to, device).wait()
+        index_copy(to).start()
+
+    def send_block(step):
+        to, _, device = partner(step)
+        index_copy(to).wait()
         leaving[to] = gather_block(to)
         row_copy(to, me, device).start()
 
-    for_partners(send_block)
+    def send_ahead(step, carry):
+        fetch_request(step + 1)
+        send_block(step)
+        return carry
+
+    index_copy(me).start()
+    fetch_request(0)
+    lax.fori_loop(0, count - 2, send_ahead, 0)
+    send_block(count - 2)
+    index_copy(me).wait()
     arrived[me] = gather_block(me)
 
     for load in loads[2:]:
@@ -366,7 +380,7 @@
             pltpu.VMEM((features, features), f32),
             pltpu.VMEM((2 * user_count, features), f32),
             pltpu.VMEM((user_count, features), f32),
-            dma((5,)), dma, dma,
+            dma((5,)), dma, dma((devices,)),
             dma((2, devices)), dma((2, devices)), dma((2, devices)), dma((2, devices)),
         ],
         compiler_params=pltpu.CompilerParams(

time: 81.9 us -> 80 us (0.977)
  Pallas kernels: 80.3 us -> 78.4 us
    pallas_call x1, Pallas kernels: 80.3 us -> 78.4 us  [per_device(): pl.pallas_call(functools.partial(sweep_kernel, total_items), out_shape=ja...]
where the time goes in v6:
time: 80 us; the launch traced here: 79.8 us
  Pallas kernels  78.4 us (98%)
  local copies, waits for them, and re-layouts  1.38 us (2%)
    pallas_call x1, Pallas kernels, per_device(): pl.pallas_call(functools.partial(sweep_kernel, total_items), out_shape=ja...  78.4 us

profile of v6, /device:TPU:0, one launch (start us, length us, event | category | flops | bytes accessed | tf_op | source)
XLA Modules:
  0.0 79.8 jit_solution(2264135646722804515)
XLA Ops:
  0.0 78.4 %sweep.1 = f32[64,128]{1,0:T(8,128)} custom-call(s32[64]{0:T(128)} %counts_hbm.1, bf16[16384,128]{1,0:T(8,128)(2,1)} %table_hbm.1, s32[64,128]{1,0:T(8,128)} %slots_hbm.1, s32[64,128]{1,0:T(8,128)} %rows_hbm.1, s32[64,128]{1,0:T(8,128)} %weights_hbm.1, f32[64,128]{1,0:T(8,128)} %start_hbm.1), custom_call_target="tpu_custom_call" | custom-call | tf_op jit(solution)/shard_map/sweep/pallas_call | solution.py:354
  78.4 1.4 %copy.8 = f32[64,128]{1,0:T(8,128)} copy(f32[64,128]{1,0:T(8,128)} %sweep.1) | data formatting | bytes 65536

commit v7 on v6

--- a/solution.py
+++ b/solution.py
@@ -200,7 +200,27 @@
 
     index_copy(me).start()
     fetch_request(0)
-    lax.fori_loop(0, count - 2, send_ahead, 0)
+    lax.fori_loop(0, 4, send_ahead, 0)
+
+    def gramian(index, total):
+        at = pl.ds(pl.multiple_of(index * chunk, chunk), chunk)
+        block = table[at, :]
+        return total + lax.dot_general(block, block, TN, preferred_element_type=f32)
+
+    own = lax.fori_loop(
+        0, table.shape[0] // chunk, gramian, jnp.zeros((features, features), f32)
+    )
+    for index in range(count):
+        parts[index] = own[index * share:(index + 1) * share]
+    for_partners(lambda to, source, device: part_copy(to, me, device).start())
+    partial[me] = parts[me]
+
+    lax.fori_loop(4, count // 2, send_ahead, 0)
+    for_partners(finish(part_copy))
+    summed[...] = jnp.sum(partial[...], axis=0)
+    for_partners(lambda to, source, device: whole_copy(to, me, device).start())
+    whole[me] = summed[...]
+    lax.fori_loop(count // 2, count - 2, send_ahead, 0)
     send_block(count - 2)
     index_copy(me).wait()
     arrived[me] = gather_block(me)
@@ -229,19 +249,6 @@
         return carry
 
     lax.fori_loop(0, count, mark, 0)
-
-    def gramian(index, total):
-        at = pl.ds(pl.multiple_of(index * chunk, chunk), chunk)
-        block = table[at, :]
-        return total + lax.dot_general(block, block, TN, preferred_element_type=f32)
-
-    own = lax.fori_loop(
-        0, table.shape[0] // chunk, gramian, jnp.zeros((features, features), f32)
-    )
-    for index in range(count):
-        parts[index] = own[index * share:(index + 1) * share]
-    for_partners(lambda to, source, device: part_copy(to, me, device).start())
-    partial[me] = parts[me]
 
     def products(owner, vector_parts, total, weighted):
         inner = lax.dot_general(vector_parts, arrived[owner], NT, preferred_element_type=f32)
@@ -285,12 +292,7 @@
     take_blocks([me])
     receive_blocks([0])
     pairs = (count - 2) // 2
-    lax.fori_loop(0, pairs // 2, receive_pair, 0)
-    for_partners(finish(part_copy))
-    summed[...] = jnp.sum(partial[...], axis=0)
-    for_partners(lambda to, source, device: whole_copy(to, me, device).start())
-    whole[me] = summed[...]
-    lax.fori_loop(pairs // 2, pairs, receive_pair, 0)
+    lax.fori_loop(0, pairs, receive_pair, 0)
     for_partners(finish(whole_copy))
 
     for index in range(count):

time: 80 us -> 76.4 us (0.955)
  Pallas kernels: 78.4 us -> 74.8 us
    pallas_call x1, Pallas kernels: 78.4 us -> 74.8 us  [per_device(): pl.pallas_call(functools.partial(sweep_kernel, total_items), out_shape=ja...]
where the time goes in v7:
time: 76.4 us; the launch traced here: 76.2 us
  Pallas kernels  74.8 us (98%)
  local copies, waits for them, and re-layouts  1.38 us (2%)
    pallas_call x1, Pallas kernels, per_device(): pl.pallas_call(functools.partial(sweep_kernel, total_items), out_shape=ja...  74.8 us

profile of v7, /device:TPU:0, one launch (start us, length us, event | category | flops | bytes accessed | tf_op | source)
XLA Modules:
  0.0 76.2 jit_solution(2070783971808305613)
XLA Ops:
  0.0 74.8 %sweep.1 = f32[64,128]{1,0:T(8,128)} custom-call(s32[64]{0:T(128)} %counts_hbm.1, bf16[16384,128]{1,0:T(8,128)(2,1)} %table_hbm.1, s32[64,128]{1,0:T(8,128)} %slots_hbm.1, s32[64,128]{1,0:T(8,128)} %rows_hbm.1, s32[64,128]{1,0:T(8,128)} %weights_hbm.1, f32[64,128]{1,0:T(8,128)} %start_hbm.1), custom_call_target="tpu_custom_call" | custom-call | tf_op jit(solution)/shard_map/sweep/pallas_call | solution.py:356
  74.8 1.4 %copy.8 = f32[64,128]{1,0:T(8,128)} copy(f32[64,128]{1,0:T(8,128)} %sweep.1) | data formatting | bytes 65536

commit v8 on v7

--- a/solution.py
+++ b/solution.py
@@ -8,6 +8,7 @@
 from jax.sharding import PartitionSpec as P
 
 CG_STEPS = 3
+PLACED = 32
 MESH = pl.DeviceIdType.MESH
 VMEM_BYTES = 64 * 1024 * 1024 - 65536
 NT = (((1,), (1,)), ((), ()))
@@ -53,7 +54,7 @@
 def place(slots_ref, read_parts, owners, capacity):
     users, width = slots_ref.shape
     shift = capacity.bit_length() - 1
-    group = 8
+    group = PLACED
 
     def one_group(index, total):
         at = pl.ds(pl.multiple_of(index * group, group), group)
@@ -229,7 +230,7 @@
         load.wait()
 
     def link_parts(first, at):
-        shape = (8, slot_count)
+        shape = (PLACED, slot_count)
         line = lax.broadcasted_iota(jnp.int32, shape, 0)
         limit = jnp.zeros(shape, jnp.int32)
         for j in range(shape[0]):

time: 76.4 us -> 76.3 us (level)
  no operation moved by 1% of the time
where the time goes in v8:
time: 76.3 us; the launch traced here: 76.2 us
  Pallas kernels  74.8 us (98%)
  local copies, waits for them, and re-layouts  1.38 us (2%)
    pallas_call x1, Pallas kernels, per_device(): pl.pallas_call(functools.partial(sweep_kernel, total_items), out_shape=ja...  74.8 us

profile of v8, /device:TPU:0, one launch (start us, length us, event | category | flops | bytes accessed | tf_op | source)
XLA Modules:
  0.0 76.2 jit_solution(2915453411426449600)
XLA Ops:
  0.0 74.8 %sweep.1 = f32[64,128]{1,0:T(8,128)} custom-call(s32[64]{0:T(128)} %counts_hbm.1, bf16[16384,128]{1,0:T(8,128)(2,1)} %table_hbm.1, s32[64,128]{1,0:T(8,128)} %slots_hbm.1, s32[64,128]{1,0:T(8,128)} %rows_hbm.1, s32[64,128]{1,0:T(8,128)} %weights_hbm.1, f32[64,128]{1,0:T(8,128)} %start_hbm.1), custom_call_target="tpu_custom_call" | custom-call | tf_op jit(solution)/shard_map/sweep/pallas_call | solution.py:357
  74.8 1.4 %copy.8 = f32[64,128]{1,0:T(8,128)} copy(f32[64,128]{1,0:T(8,128)} %sweep.1) | data formatting | bytes 65536
